TPU v7x, 32 devices: a whole 2x2x4 slice. The times are simulated.
32 devices in a mesh: row: 8 (over z, x), col: 4 (over y, core).
Axes of the slice: x: 2, y: 2, z: 4, core: 2. Of those that a mesh axis runs over, the one named last changes fastest.
Arguments:
- features: bfloat16 [4096, 1024], P(('col', 'row')), may hold values from -6 to 6
- weight: bfloat16 [1024, 1024], P('col'), may hold values from -0.1875 to 0.1875
- tile_values: bfloat16 [8, 4, 4, 8, 128, 128], P('row', 'col'), may hold values from -0.125 to 0.125
- block_cols: int32 [8, 4, 4, 8], P('row', 'col'), may hold values from 0 to 7, as said below
- tile_counts: int32 [8, 4, 4], P('row', 'col'), may hold values from 1 to 8, as said below
Outputs:
- hidden_out: bfloat16 [4096, 1024], P(('row', 'col'))
Inputs may be any that keep to these rules, and one draw needn't show every extreme that they name: `block_cols`: the 8 entries of one block row of a tile are distinct block columns; values and block columns of slots that are not live are arbitrary. `tile_counts`: every tile has a block row with all 8 slots live.
All inputs are finite; a program needn't handle non-finite values.
Results may differ from a plain program's by a relative error of at most 0.019.
Values may be sent and summed in bfloat16 or wider, within the bound.
A program may use at most 64 MiB of HBM per device.

v0:
```python
from functools import partial

import jax
import jax.numpy as jnp
from jax import lax
from jax.sharding import PartitionSpec as P


def aggregate(slot_values, slot_cols, slot_count, column_rows, group_size, offset, row_span):
    block_size = slot_values.shape[-1]
    slot_total = slot_values.shape[1]
    feat_width = column_rows.shape[-1]
    by_block = column_rows.reshape(-1, block_size, feat_width)
    row_count = row_span // block_size
    values_part = slot_values
    cols_part = slot_cols
    count_part = slot_count
    groups = row_count // group_size
    values_part = values_part.reshape(groups, group_size, slot_total, block_size, block_size)
    cols_part = cols_part.reshape(groups, group_size, slot_total)
    count_part = count_part.reshape(groups, group_size)

    def one_group(group_args):
        group_values, group_cols, group_count = group_args
        gathered = by_block[group_cols]
        live_slots = jnp.arange(slot_total, dtype=jnp.int32)[None, :] < group_count[:, None]
        masked = jnp.where(live_slots[:, :, None, None], group_values, jnp.zeros_like(group_values))
        return jnp.einsum("rsab,rsbf->raf", masked, gathered, preferred_element_type=jnp.float32)

    result = lax.map(one_group, (values_part, cols_part, count_part))
    return result.reshape(row_span, feat_width)


def body(features, weight, tile_values, block_cols, tile_counts):
    slot_values = tile_values[0, 0]
    slot_cols = block_cols[0, 0]
    slot_count = tile_counts[0, 0]
    out_rows = features.shape[0]
    block_size = slot_values.shape[-1]
    group_size = out_rows // block_size
    column_rows = lax.all_gather(features, "row", axis=0, tiled=True)
    partial_term = partial(aggregate, slot_values, slot_cols, slot_count, column_rows, group_size)
    summed = lax.psum_scatter(
        partial_term(jnp.int32(0), lax.axis_size("col") * out_rows).astype(jnp.bfloat16),
        "col",
        scatter_dimension=0,
        tiled=True,
    )
    product = jnp.dot(
        summed,
        lax.all_gather(weight, "col", axis=0, tiled=True),
        preferred_element_type=jnp.float32,
    )
    return jnp.maximum(product, 0.0).astype(jnp.bfloat16)


def solution(mesh):
    in_specs = (
        P(("col", "row"), None),
        P("col", None),
        P("row", "col", None, None, None, None),
        P("row", "col", None, None),
        P("row", "col", None),
    )
    out_specs = P(("row", "col"), None)
    return jax.shard_map(body, mesh=mesh, in_specs=in_specs, out_specs=out_specs, check_vma=False)
```

profile of v0, /device:TPU:0, one launch (start us, length us, event | category | flops | bytes accessed | tf_op | source)
XLA Modules:
  0.0 121.0 jit_solution(16955282499855933309)
XLA Ops:
  6.5 0.0 all-gather.3.cloned.1.call-start
  6.5 0.7 all-gather.3.cloned.1.call-update
  7.3 0.0 all-gather.5.cloned.1.call-start
  7.3 0.7 all-gather.5.cloned.1.call-update
  8.0 0.0 reduce-scatter.2.cloned.1.call-start
  8.1 53.4 %all-gather.3.cloned.1.call-done = bf16[1024,1024]{1,0:T(8,128)(2,1)} async-done(((bf16[128,1024]{1,0:T(8,128)(2,1)}), bf16[1024,1024]{1,0:T(8,128)(2,1)}) %all-gather.3.cloned.1.call-update) | async-done | bytes 2097168 | tf_op jit(solution)/shard_map/all_gather | solution.py:41
  61.5 22.5 %while.10 = (s32[]{:T(128)}, bf16[4,1,128,1024]{3,2,1,0:T(8,128)(2,1)S(1)}, s32[4,1]{0,1:T(1,128)}, bf16[4,1,8,128,128]{4,3,2,1,0:T(8,128)(2,1)}, s32[4,1,8]{2,1...) while((s32[]{:T(128)}, bf16[4,1,128,1024]{3,2,1,0:T(8,128)(2,1)S(1)}, s32[4,1]{0,1:T(1,128)}, ...), condition=%wide.region_1.2_spmd, body=%wide.region_0.1_spmd.sunk | while | flops 268567584 | bytes 7083845 | solution.py:30
  61.5 0.7 fusion.16
  62.2 0.0 copy-start.1
  62.2 2.3 %gather_fusion = bf16[8,128,1024]{2,1,0:T(8,128)(2,1)S(1)} fusion(bf16[8,128,1024]{2,1,0:T(8,128)(2,1)} %get-tuple-element.112, s32[1024]{0:T(1024)S(1)} %pad_clamp_fusion.2), kind=kCustom, calls=%fused_computation.clone.1 | custom fusion | bytes 4194336 | tf_op jit(solution)/shard_map/while/body/eval_jaxpr/gather | solution.py:25
  64.5 0.0 copy-done.1
  64.5 0.6 constant_dynamic-slice_fusion.3
  65.1 0.6 iota_compare_fusion.2
  65.6 1.4 %fusion.17 = bf16[4,1,128,1024]{3,2,1,0:T(8,128)(2,1)S(1)} fusion(bf16[4,1,128,1024]{3,2,1,0:T(8,128)(2,1)S(1)} %get-tuple-element.101, s32[]{:T(128)} %get-tuple-element.100, bf16[8,128,1024]{2,1,0:T(8,128)(2,1)S(1)} %gather_fusion, bf16[4,1,8,128,128]{4,3,2,1,0:T(8,128)(2,1)} %get-tuple-element.110, pred[8]{0:T(512)(128)(4,1)S(1)} %iota_compare_fusion.2), kind=kOutput, calls=%fused_computation.2.clone.1 | convolution fusion | flops 268566528 | bytes 2885120 | tf_op jit(solution)/shard_map/while/body/eval_jaxpr/rsab,rsbf->raf/dot_general | solution.py:28
  67.1 0.7 fusion.16
  67.8 0.0 copy-start.1
  67.8 2.4 %gather_fusion = bf16[8,128,1024]{2,1,0:T(8,128)(2,1)S(1)} fusion(bf16[8,128,1024]{2,1,0:T(8,128)(2,1)} %get-tuple-element.112, s32[1024]{0:T(1024)S(1)} %pad_clamp_fusion.2), kind=kCustom, calls=%fused_computation.clone.1 | custom fusion | bytes 4194336 | tf_op jit(solution)/shard_map/while/body/eval_jaxpr/gather | solution.py:25
  70.2 0.0 copy-done.1
  70.2 0.6 constant_dynamic-slice_fusion.3
  70.8 0.6 iota_compare_fusion.2
  71.3 1.4 %fusion.17 = bf16[4,1,128,1024]{3,2,1,0:T(8,128)(2,1)S(1)} fusion(bf16[4,1,128,1024]{3,2,1,0:T(8,128)(2,1)S(1)} %get-tuple-element.101, s32[]{:T(128)} %get-tuple-element.100, bf16[8,128,1024]{2,1,0:T(8,128)(2,1)S(1)} %gather_fusion, bf16[4,1,8,128,128]{4,3,2,1,0:T(8,128)(2,1)} %get-tuple-element.110, pred[8]{0:T(512)(128)(4,1)S(1)} %iota_compare_fusion.2), kind=kOutput, calls=%fused_computation.2.clone.1 | convolution fusion | flops 268566528 | bytes 2885120 | tf_op jit(solution)/shard_map/while/body/eval_jaxpr/rsab,rsbf->raf/dot_general | solution.py:28
  72.8 0.7 fusion.16
  73.5 0.0 copy-start.1
  73.5 2.3 %gather_fusion = bf16[8,128,1024]{2,1,0:T(8,128)(2,1)S(1)} fusion(bf16[8,128,1024]{2,1,0:T(8,128)(2,1)} %get-tuple-element.112, s32[1024]{0:T(1024)S(1)} %pad_clamp_fusion.2), kind=kCustom, calls=%fused_computation.clone.1 | custom fusion | bytes 4194336 | tf_op jit(solution)/shard_map/while/body/eval_jaxpr/gather | solution.py:25
  75.8 0.0 copy-done.1
  75.8 0.6 constant_dynamic-slice_fusion.3
  76.4 0.6 iota_compare_fusion.2
  76.9 1.4 %fusion.17 = bf16[4,1,128,1024]{3,2,1,0:T(8,128)(2,1)S(1)} fusion(bf16[4,1,128,1024]{3,2,1,0:T(8,128)(2,1)S(1)} %get-tuple-element.101, s32[]{:T(128)} %get-tuple-element.100, bf16[8,128,1024]{2,1,0:T(8,128)(2,1)S(1)} %gather_fusion, bf16[4,1,8,128,128]{4,3,2,1,0:T(8,128)(2,1)} %get-tuple-element.110, pred[8]{0:T(512)(128)(4,1)S(1)} %iota_compare_fusion.2), kind=kOutput, calls=%fused_computation.2.clone.1 | convolution fusion | flops 268566528 | bytes 2885120 | tf_op jit(solution)/shard_map/while/body/eval_jaxpr/rsab,rsbf->raf/dot_general | solution.py:28
  78.4 0.7 fusion.16
  79.1 0.0 copy-start.1
  79.1 2.3 %gather_fusion = bf16[8,128,1024]{2,1,0:T(8,128)(2,1)S(1)} fusion(bf16[8,128,1024]{2,1,0:T(8,128)(2,1)} %get-tuple-element.112, s32[1024]{0:T(1024)S(1)} %pad_clamp_fusion.2), kind=kCustom, calls=%fused_computation.clone.1 | custom fusion | bytes 4194336 | tf_op jit(solution)/shard_map/while/body/eval_jaxpr/gather | solution.py:25
  81.4 0.0 copy-done.1
  81.4 0.6 constant_dynamic-slice_fusion.3
  82.0 0.6 iota_compare_fusion.2
  82.5 1.4 %fusion.17 = bf16[4,1,128,1024]{3,2,1,0:T(8,128)(2,1)S(1)} fusion(bf16[4,1,128,1024]{3,2,1,0:T(8,128)(2,1)S(1)} %get-tuple-element.101, s32[]{:T(128)} %get-tuple-element.100, bf16[8,128,1024]{2,1,0:T(8,128)(2,1)S(1)} %gather_fusion, bf16[4,1,8,128,128]{4,3,2,1,0:T(8,128)(2,1)} %get-tuple-element.110, pred[8]{0:T(512)(128)(4,1)S(1)} %iota_compare_fusion.2), kind=kOutput, calls=%fused_computation.2.clone.1 | convolution fusion | flops 268566528 | bytes 2885120 | tf_op jit(solution)/shard_map/while/body/eval_jaxpr/rsab,rsbf->raf/dot_general | solution.py:28
  84.0 0.0 copy-start
  84.0 1.0 copy-done
  85.0 0.0 reduce-scatter.2.cloned.1.call-update
  85.0 0.0 all-gather.5.cloned.1.call-done
  85.0 26.6 %reduce-scatter.2.cloned.1.call-done = bf16[128,1024]{1,0:T(8,128)(2,1)} async-done(((bf16[512,1024]{1,0:T(8,128)(2,1)}), bf16[128,1024]{1,0:T(8,128)(2,1)}) %reduce-scatter.2.cloned.1.call-update) | async-done | bytes 262160 | tf_op jit(solution)/shard_map/reduce_scatter | solution.py:43
  111.6 2.8 %fusion.8 = bf16[128,1024]{1,0:T(8,128)(2,1)} fusion(bf16[128,1024]{1,0:T(8,128)(2,1)} %reduce-scatter.2.cloned.1.call-done, bf16[1024,1024]{1,0:T(8,128)(2,1)} %all-gather.5.cloned.1.call-done), kind=kOutput, calls=%fused_computation.17 | convolution fusion | flops 268697600 | bytes 2621440 | tf_op jit(solution)/shard_map/dot_general | solution.py:49
  (5 shorter events, 0.0 us)
Async XLA Ops:
  6.5 55.0 %all-gather.3.cloned.1.call-start = ((), (), s32[]{:S(2)}) async-start(), calls=%async_computation.1 | async-start | bytes 2359296 | tf_op jit(solution)/shard_map/all_gather | solution.py:41
  7.3 77.8 %all-gather.5.cloned.1.call-start = ((), (), s32[]{:S(2)}) async-start(), calls=%async_computation.3 | async-start | bytes 2621440 | tf_op jit(solution)/shard_map/all_gather | solution.py:51
  8.0 103.6 %reduce-scatter.2.cloned.1.call-start = ((), (), s32[]{:S(2)}) async-start(), calls=%async_computation.2 | async-start | bytes 1310720 | tf_op jit(solution)/shard_map/reduce_scatter | solution.py:43
  62.2 2.3 %copy-start.1 = (s32[4,1]{0,1:T(1,128)S(1)}, s32[4,1]{0,1:T(1,128)}, u32[]{:S(2)}) copy-start(s32[4,1]{0,1:T(1,128)} %get-tuple-element.109) | copy-start | bytes 52 | tf_op jit(solution)/shard_map/while
  67.8 2.4 %copy-start.1 = (s32[4,1]{0,1:T(1,128)S(1)}, s32[4,1]{0,1:T(1,128)}, u32[]{:S(2)}) copy-start(s32[4,1]{0,1:T(1,128)} %get-tuple-element.109) | copy-start | bytes 52 | tf_op jit(solution)/shard_map/while
  73.5 2.3 %copy-start.1 = (s32[4,1]{0,1:T(1,128)S(1)}, s32[4,1]{0,1:T(1,128)}, u32[]{:S(2)}) copy-start(s32[4,1]{0,1:T(1,128)} %get-tuple-element.109) | copy-start | bytes 52 | tf_op jit(solution)/shard_map/while
  79.1 2.3 %copy-start.1 = (s32[4,1]{0,1:T(1,128)S(1)}, s32[4,1]{0,1:T(1,128)}, u32[]{:S(2)}) copy-start(s32[4,1]{0,1:T(1,128)} %get-tuple-element.109) | copy-start | bytes 52 | tf_op jit(solution)/shard_map/while
  84.0 1.0 copy-start
Sparse Core Ops, SparseCore 0:
  9.5 51.9 all-gather.2
  63.1 21.0 all-gather.4
  86.7 24.8 reduce-scatter.1
where the time goes:
time: 121 us
  waiting for transfers between devices  81.4 us (67%)
  between operations  13.1 us (11%)
  local copies, waits for them, and re-layouts  12.6 us (10%)
  matrix products  8.62 us (7%)
  other arithmetic  4.92 us (4%)
    all_gather x1, waiting for transfers between devices, body(): column_rows = lax.all_gather(features, 'row', axis=0, tiled=True)  53.4 us
    reduce_scatter x1, waiting for transfers between devices, body(): lax.psum_scatter(partial_term(jnp.int32(0), lax.axis_size('col') * out_ro...  26.6 us
    gather x4, local copies, waits for them, and re-layouts, one_group(): gathered = by_block[group_cols]  9.28 us
    dot_general x4, matrix products, one_group(): jnp.einsum('rsab,rsbf->raf', masked, gathered, preferred_element_type=jnp...  5.78 us
    dot_general x1, matrix products, body(): jnp.dot(summed, lax.all_gather(weight, 'col', axis=0, tiled=True), prefer...  2.84 us
    select_n x4, other arithmetic, one_group(): gathered = by_block[group_cols]  2.64 us
  transfers between devices with their start and end apart: 3, of which 2 were waited for; matrix products, arithmetic and copies ran while one was open for 18% of the time, Pallas kernels for 0%

commit v1 on v0

v1 whole, which is shorter than its diff:
```python
import functools

import jax
import jax.numpy as jnp
from jax import lax
from jax.experimental import pallas as pl
from jax.experimental.pallas import tpu as pltpu
from jax.sharding import PartitionSpec as P

MESH = pl.DeviceIdType.MESH
CHUNKS = 4


def kernel(rows_n, cols_n, x_n, cols_ref, counts_ref, feat_ref, weight_ref, vals_ref, out_ref,
           gath, wfull, vals, dense, psend, psib, ssum, ssend, srecv, acc,
           local_sem, zsend_sem, xsend_sem, grecv_sem, wsend_sem, wfwd_sem, wrecv_sem,
           psend_sem, precv_sem, ssend_sem, srecv_sem):
    z_n = rows_n // x_n
    q_n = cols_n // 2
    row = lax.axis_index("row")
    col = lax.axis_index("col")
    z, x = row // x_n, row % x_n
    q, core = col // 2, col % 2
    other = 1 - core
    sib = q * 2 + other
    row_blk, slots, bs = vals.shape[0], vals.shape[1], vals.shape[2]
    col_blk = rows_n
    out_rows = feat_ref.shape[0]
    feat = feat_ref.shape[1]
    fc = feat // CHUNKS
    wr = weight_ref.shape[0]

    z_steps = sorted(range(1, z_n), key=lambda d: min(d, z_n - d))
    z_to = [((z + d) % z_n) * x_n + x for d in z_steps]
    z_from = [((z + z_n - d) % z_n) * x_n + x for d in z_steps]
    x_steps = list(range(1, x_n))
    q_steps = list(range(1, q_n))
    q_to = [((q + d) % q_n) for d in q_steps]
    q_from = [((q + q_n - d) % q_n) for d in q_steps]

    local = [
        pltpu.make_async_copy(vals_ref.at[0, 0], vals, local_sem.at[0]),
        pltpu.make_async_copy(weight_ref, wfull.at[pl.ds(pl.multiple_of(col * wr, wr), wr)], local_sem.at[1]),
    ]
    for c in range(CHUNKS):
        local.append(pltpu.make_async_copy(
            feat_ref.at[:, pl.ds(c * fc, fc)], gath.at[c, row], local_sem.at[2 + c]))
    for copy in local:
        copy.start()

    barrier = pltpu.get_barrier_semaphore()
    peers = 0
    for r in z_to + [z * x_n + (x + d) % x_n for d in x_steps]:
        pl.semaphore_signal(barrier, inc=1, device_id={"row": r, "col": col}, device_id_type=MESH)
        peers += 1
    for j in [t * 2 + core for t in q_to] + [sib]:
        pl.semaphore_signal(barrier, inc=1, device_id={"row": row, "col": j}, device_id_type=MESH)
        peers += 1
    pl.semaphore_wait(barrier, peers)

    sends = []

    def send(src, dst, ssem, rsem, r, j):
        copy = pltpu.make_async_remote_copy(
            src_ref=src, dst_ref=dst, send_sem=ssem, recv_sem=rsem,
            device_id={"row": r, "col": j}, device_id_type=MESH)
        copy.start()
        sends.append(copy)

    def arrived(ref, sem):
        pltpu.make_async_copy(ref, ref, sem).wait()

    def x_send(c, origin, n, src):
        for k, d in enumerate(x_steps):
            send(src, gath.at[c, origin], xsend_sem.at[c, n, k], grecv_sem.at[c, origin],
                 z * x_n + (x + d) % x_n, col)

    for c in range(CHUNKS):
        src = feat_ref.at[:, pl.ds(c * fc, fc)]
        for k, r in enumerate(z_to):
            send(src, gath.at[c, row], zsend_sem.at[c, k], grecv_sem.at[c, row], r, col)
        x_send(c, row, 0, src)

    wmine = pl.ds(pl.multiple_of(col * wr, wr), wr)
    for k, t in enumerate(q_to):
        send(weight_ref, wfull.at[wmine], wsend_sem.at[k], wrecv_sem.at[col], row, t * 2 + core)
    send(weight_ref, wfull.at[wmine], wfwd_sem.at[0], wrecv_sem.at[col], row, sib)

    local[0].wait()

    def make_dense(r, carry):
        count = counts_ref[0, 0, r]
        ids = [cols_ref[0, 0, r, s] for s in range(slots)]
        for c in range(col_blk):
            slot = jnp.int32(0)
            live = jnp.int32(0)
            for s in range(slots):
                hit = jnp.logical_and(ids[s] == c, s < count)
                slot = jnp.where(hit, s, slot)
                live = jnp.where(hit, 1, live)
            block = vals[r, slot]
            dense[r % 2, r // 2, :, c * bs:(c + 1) * bs] = jnp.where(live == 1, block, jnp.zeros_like(block))
        return carry

    lax.fori_loop(0, row_blk, make_dense, 0)

    def forward(c):
        for n, r in enumerate(z_from):
            arrived(gath.at[c, r], grecv_sem.at[c, r])
            x_send(c, r, n + 1, gath.at[c, r])

    def w_forward():
        for k, t in enumerate(q_from):
            part = pl.ds(pl.multiple_of((t * 2 + core) * wr, wr), wr)
            arrived(wfull.at[part], wrecv_sem.at[t * 2 + core])
            send(wfull.at[part], wfull.at[part], wfwd_sem.at[k + 1], wrecv_sem.at[t * 2 + core], row, sib)

    def w_arrive():
        local[1].wait()
        for t in range(q_n):
            j = t * 2 + other
            part = pl.ds(pl.multiple_of(j * wr, wr), wr)
            arrived(wfull.at[part], wrecv_sem.at[j])

    per = max(1, min(q_n, 256 // out_rows))

    def aggregate(c):
        local[2 + c].wait()
        for d in x_steps:
            for zz in range(z_n):
                r = zz * x_n + (x + d) % x_n
                arrived(gath.at[c, r], grecv_sem.at[c, r])

        def dots(which, put):
            def step(t, carry):
                a = dense[which, pl.ds(t * per, per)].reshape(per * out_rows, col_blk * bs)
                g = gath[c].reshape(col_blk * bs, fc)
                put(t, jnp.dot(a, g, preferred_element_type=jnp.float32).reshape(per, out_rows, fc))
                return carry
            if q_n == per:
                step(0, 0)
            else:
                lax.fori_loop(0, q_n // per, step, 0)

        def put_send(t, v):
            psend[c, pl.ds(t * per, per)] = v.astype(psend.dtype)

        def put_sum(t, v):
            ssum[c, pl.ds(t * per, per)] = v

        dots(other, put_send)
        send(psend.at[c], psib.at[c], psend_sem.at[c], precv_sem.at[c], row, sib)
        dots(core, put_sum)

    def pair_sum(c):
        arrived(psib.at[c], precv_sem.at[c])
        total = ssum[c] + psib[c].astype(jnp.float32)
        ssum[c] = total
        ssend[c] = total.astype(ssend.dtype)
        for k, t in enumerate(q_to):
            send(ssend.at[c, t], srecv.at[c, q], ssend_sem.at[c, k], srecv_sem.at[c, q], row, t * 2 + core)

    def finish(c):
        total = ssum[c, q]
        for t in q_from:
            arrived(srecv.at[c, t], srecv_sem.at[c, t])
            total = total + srecv[c, t].astype(jnp.float32)
        part = jnp.dot(total.astype(jnp.bfloat16), wfull[c * fc:(c + 1) * fc, :],
                       preferred_element_type=jnp.float32)
        if c == 0:
            acc[...] = part
        elif c < CHUNKS - 1:
            acc[...] += part
        else:
            out_ref[...] = jnp.maximum(acc[...] + part, 0.0).astype(out_ref.dtype)

    forward(0)
    for step in range(1, CHUNKS + 4):
        if step < CHUNKS:
            forward(step)
        if step == 2:
            w_forward()
        if 0 <= step - 1 < CHUNKS:
            aggregate(step - 1)
        if 0 <= step - 2 < CHUNKS:
            pair_sum(step - 2)
        if step == 3:
            w_arrive()
        if 0 <= step - 3 < CHUNKS:
            finish(step - 3)
    for copy in sends:
        copy.wait_send()


def solution(mesh):
    rows_n, cols_n = mesh.shape["row"], mesh.shape["col"]
    x_n = 1 << ((rows_n.bit_length() - 1) // 2)
    z_n = rows_n // x_n
    q_n = cols_n // 2

    def body(features, weight, tile_values, block_cols, tile_counts):
        out_rows, feat = features.shape
        _, _, row_blk, slots, bs, _ = tile_values.shape
        fc = feat // CHUNKS
        wide = weight.shape[1]
        dma = pltpu.SemaphoreType.DMA
        bf16, f32 = jnp.bfloat16, jnp.float32
        flops = 2 * row_blk * bs * rows_n * bs * feat + 2 * out_rows * feat * wide
        return pl.pallas_call(
            functools.partial(kernel, rows_n, cols_n, x_n),
            out_shape=jax.ShapeDtypeStruct((out_rows, wide), bf16),
            in_specs=[pl.BlockSpec(memory_space=pltpu.SMEM)] * 2 + [pl.BlockSpec(memory_space=pl.ANY)] * 3,
            out_specs=pl.BlockSpec(memory_space=pltpu.VMEM),
            scratch_shapes=[
                pltpu.VMEM((CHUNKS, rows_n, out_rows, fc), bf16),
                pltpu.VMEM((feat, wide), bf16),
                pltpu.VMEM((row_blk, slots, bs, bs), bf16),
                pltpu.VMEM((2, q_n, out_rows, rows_n * bs), bf16),
                pltpu.VMEM((CHUNKS, q_n, out_rows, fc), bf16),
                pltpu.VMEM((CHUNKS, q_n, out_rows, fc), bf16),
                pltpu.VMEM((CHUNKS, q_n, out_rows, fc), f32),
                pltpu.VMEM((CHUNKS, q_n, out_rows, fc), bf16),
                pltpu.VMEM((CHUNKS, q_n, out_rows, fc), bf16),
                pltpu.VMEM((out_rows, wide), f32),
                dma((2 + CHUNKS,)),
                dma((CHUNKS, max(1, z_n - 1))),
                dma((CHUNKS, z_n, max(1, x_n - 1))),
                dma((CHUNKS, rows_n)),
                dma((max(1, q_n - 1),)),
                dma((q_n,)),
                dma((cols_n,)),
                dma((CHUNKS,)),
                dma((CHUNKS,)),
                dma((CHUNKS, max(1, q_n - 1))),
                dma((CHUNKS, q_n)),
            ],
            compiler_params=pltpu.CompilerParams(
                collective_id=0, has_side_effects=True, vmem_limit_bytes=48 * 1024 * 1024),
            cost_estimate=pl.CostEstimate(flops=flops, bytes_accessed=4 * 1024 * 1024, transcendentals=0),
        )(block_cols, tile_counts, features, weight, tile_values)

    in_specs = (
        P(("col", "row"), None),
        P("col", None),
        P("row", "col", None, None, None, None),
        P("row", "col", None, None),
        P("row", "col", None),
    )
    return jax.shard_map(body, mesh=mesh, in_specs=in_specs, out_specs=P(("row", "col"), None), check_vma=False)
```

time: 121 us -> 47.8 us (0.40)
  waiting for transfers between devices: 81.4 us -> 0 us
  Pallas kernels: 0 us -> 42.3 us
  between operations: 13.1 us -> 0.01 us
  matrix products: 8.62 us -> 0 us
  local copies, waits for them, and re-layouts: 12.6 us -> 5.26 us
  other arithmetic: 4.92 us -> 0 us
    all_gather x2 -> x0, waiting for transfers between devices: 53.5 us -> none  [the longest x1 53.4 us: body(): column_rows = lax.all_gather(features, 'row', axis=0, tiled=True)]
    pallas_call x0 -> x1, Pallas kernels: none -> 42.3 us  [body(): pl.pallas_call(functools.partial(kernel, rows_n, cols_n, x_n), out_shape=...]
    reduce_scatter x1 -> x0, waiting for transfers between devices: 26.6 us -> none  [body(): lax.psum_scatter(partial_term(jnp.int32(0), lax.axis_size('col') * out_ro...]
    gather x4 -> x0, local copies, waits for them, and re-layouts: 9.28 us -> none  [one_group(): gathered = by_block[group_cols]]
    dot_general x5 -> x0, matrix products: 8.62 us -> none  [the longest x4 5.78 us: one_group(): jnp.einsum('rsab,rsbf->raf', masked, gathered, preferred_element_type=jnp...]
    unnamed x2 -> x11, local copies, waits for them, and re-layouts: 0.97 us -> 5.26 us
    select_n x4 -> x0, other arithmetic: 2.64 us -> none  [one_group(): gathered = by_block[group_cols]]
    dynamic_slice x4 -> x0, local copies, waits for them, and re-layouts: 2.32 us -> none  [aggregate(): result = lax.map(one_group, (values_part, cols_part, count_part))]
  transfers between devices with their start and end apart: 3 -> 0, of which waited for: 2 -> 0; matrix products, arithmetic and copies ran while one was open for 18% -> 0% of each run, Pallas kernels for 0% -> 0%
where the time goes in v1:
time: 47.8 us; the launch traced here: 47.6 us
  Pallas kernels  42.3 us (88%)
  local copies, waits for them, and re-layouts  5.26 us (11%)
    pallas_call x1, Pallas kernels, body(): pl.pallas_call(functools.partial(kernel, rows_n, cols_n, x_n), out_shape=...  42.3 us
    unnamed x11, local copies, waits for them, and re-layouts  5.26 us

profile of v1, /device:TPU:0, one launch (start us, length us, event | category | flops | bytes accessed | tf_op | source)
XLA Modules:
  0.0 47.6 jit_solution(8645499437307885838)
XLA Ops:
  0.0 0.0 copy-start
  0.0 1.2 %copy-done = bf16[1,1,4,8,128,128]{5,4,3,2,1,0:T(8,128)(2,1)S(1)} copy-done((bf16[1,1,4,8,128,128]{5,4,3,2,1,0:T(8,128)(2,1)S(1)}, bf16[1,1,4,8,128,128]{5,4,3,2,1,0:T(8,128)(2,1)}, u32[]{:S(2)}) %copy-start) | copy-done | bytes 1048600
  1.2 0.0 copy-start.1
  1.2 1.0 %copy-done.1 = bf16[256,1024]{1,0:T(8,128)(2,1)S(1)} copy-done((bf16[256,1024]{1,0:T(8,128)(2,1)S(1)}, bf16[256,1024]{1,0:T(8,128)(2,1)}, u32[]{:S(2)}) %copy-start.1) | copy-done | bytes 524312
  2.3 0.0 copy-start.2
  2.3 0.9 %copy-done.2 = bf16[128,1024]{1,0:T(8,128)(2,1)S(1)} copy-done((bf16[128,1024]{1,0:T(8,128)(2,1)S(1)}, bf16[128,1024]{1,0:T(8,128)(2,1)}, u32[]{:S(2)}) %copy-start.2) | copy-done | bytes 262168
  3.2 0.0 copy-start.3
  3.2 0.7 %copy-done.3 = s32[1,1,4,8]{3,2,1,0:T(4,128)S(1)} copy-done((s32[1,1,4,8]{3,2,1,0:T(4,128)S(1)}, s32[1,1,4,8]{3,2,1,0:T(4,128)}, u32[]{:S(2)}) %copy-start.3) | copy-done | bytes 152
  3.9 0.0 copy-start.4
  3.9 0.7 %copy-done.4 = s32[1,1,4]{2,1,0:T(1,128)S(1)} copy-done((s32[1,1,4]{2,1,0:T(1,128)S(1)}, s32[1,1,4]{2,1,0:T(1,128)}, u32[]{:S(2)}) %copy-start.4) | copy-done | bytes 40
  4.6 42.3 %shard_map.55 = bf16[128,1024]{1,0:T(8,128)(2,1)S(1)} custom-call(s32[1,1,4,8]{3,2,1,0:T(4,128)S(1)} %copy-done.3, s32[1,1,4]{2,1,0:T(1,128)S(1)} %copy-done.4, bf16[128,1024]{1,0:T(8,128)(2,1)S(1)} %copy-done.2, bf16[256,1024]{1,0:T(8,128)(2,1)S(1)} %copy-done.1, bf16[1,1,4,8,128,128]{5,4,3,2,1,0:T(8,128)(2,1)S(1)} %copy-done), custom_call_target="tpu_custom_call" | custom-call | flops 1342177280 | bytes 4194304 | tf_op jit(solution)/shard_map/pallas_call | solution.py:209
  46.9 0.7 %copy.7 = bf16[128,1024]{1,0:T(8,128)(2,1)} copy(bf16[128,1024]{1,0:T(8,128)(2,1)S(1)} %shard_map.55) | data formatting | bytes 524288
Async XLA Ops:
  0.0 1.2 %copy-start = (bf16[1,1,4,8,128,128]{5,4,3,2,1,0:T(8,128)(2,1)S(1)}, bf16[1,1,4,8,128,128]{5,4,3,2,1,0:T(8,128)(2,1)}, u32[]{:S(2)}) copy-start(bf16[1,1,4,8,128,128]{5,4,3,2,1,0:T(8,128)(2,1)} %vals_ref.1) | copy-start | bytes 3145732
  1.2 1.0 %copy-start.1 = (bf16[256,1024]{1,0:T(8,128)(2,1)S(1)}, bf16[256,1024]{1,0:T(8,128)(2,1)}, u32[]{:S(2)}) copy-start(bf16[256,1024]{1,0:T(8,128)(2,1)} %weight_ref.1) | copy-start | bytes 1572868
  2.3 0.9 %copy-start.2 = (bf16[128,1024]{1,0:T(8,128)(2,1)S(1)}, bf16[128,1024]{1,0:T(8,128)(2,1)}, u32[]{:S(2)}) copy-start(bf16[128,1024]{1,0:T(8,128)(2,1)} %feat_ref.1) | copy-start | bytes 786436
  3.2 0.7 %copy-start.3 = (s32[1,1,4,8]{3,2,1,0:T(4,128)S(1)}, s32[1,1,4,8]{3,2,1,0:T(4,128)}, u32[]{:S(2)}) copy-start(s32[1,1,4,8]{3,2,1,0:T(4,128)} %cols_ref.1) | copy-start | bytes 388
  3.9 0.7 %copy-start.4 = (s32[1,1,4]{2,1,0:T(1,128)S(1)}, s32[1,1,4]{2,1,0:T(1,128)}, u32[]{:S(2)}) copy-start(s32[1,1,4]{2,1,0:T(1,128)} %counts_ref.1) | copy-start | bytes 52

commit v2 on v1

--- a/solution.py
+++ b/solution.py
@@ -9,6 +9,8 @@
 
 MESH = pl.DeviceIdType.MESH
 CHUNKS = 4
+AHEAD = 2
+LATE = 1
 
 
 def kernel(rows_n, cols_n, x_n, cols_ref, counts_ref, feat_ref, weight_ref, vals_ref, out_ref,
@@ -30,9 +32,8 @@
     fc = feat // CHUNKS
     wr = weight_ref.shape[0]
 
-    z_steps = sorted(range(1, z_n), key=lambda d: min(d, z_n - d))
-    z_to = [((z + d) % z_n) * x_n + x for d in z_steps]
-    z_from = [((z + z_n - d) % z_n) * x_n + x for d in z_steps]
+    has_up, has_down = z < z_n - 1, z > 0
+    up, down = (z + 1) * x_n + x, (z - 1) * x_n + x
     x_steps = list(range(1, x_n))
     q_steps = list(range(1, q_n))
     q_to = [((q + d) % q_n) for d in q_steps]
@@ -49,8 +50,12 @@
         copy.start()
 
     barrier = pltpu.get_barrier_semaphore()
-    peers = 0
-    for r in z_to + [z * x_n + (x + d) % x_n for d in x_steps]:
+    peers = jnp.where(has_up, 1, 0) + jnp.where(has_down, 1, 0)
+    for present, r in ((has_up, up), (has_down, down)):
+        @pl.when(present)
+        def _():
+            pl.semaphore_signal(barrier, inc=1, device_id={"row": r, "col": col}, device_id_type=MESH)
+    for r in [z * x_n + (x + d) % x_n for d in x_steps]:
         pl.semaphore_signal(barrier, inc=1, device_id={"row": r, "col": col}, device_id_type=MESH)
         peers += 1
     for j in [t * 2 + core for t in q_to] + [sib]:
@@ -60,26 +65,32 @@
 
     sends = []
 
-    def send(src, dst, ssem, rsem, r, j):
+    def send(src, dst, ssem, rsem, r, j, present=None):
         copy = pltpu.make_async_remote_copy(
             src_ref=src, dst_ref=dst, send_sem=ssem, recv_sem=rsem,
             device_id={"row": r, "col": j}, device_id_type=MESH)
-        copy.start()
-        sends.append(copy)
+        if present is None:
+            copy.start()
+        else:
+            pl.when(present)(copy.start)
+        sends.append((copy, present))
 
     def arrived(ref, sem):
         pltpu.make_async_copy(ref, ref, sem).wait()
 
-    def x_send(c, origin, n, src):
+    def x_send(c, origin, n, src, present=None):
         for k, d in enumerate(x_steps):
             send(src, gath.at[c, origin], xsend_sem.at[c, n, k], grecv_sem.at[c, origin],
-                 z * x_n + (x + d) % x_n, col)
-
-    for c in range(CHUNKS):
+                 z * x_n + (x + d) % x_n, col, present)
+
+    def own(c):
         src = feat_ref.at[:, pl.ds(c * fc, fc)]
-        for k, r in enumerate(z_to):
-            send(src, gath.at[c, row], zsend_sem.at[c, k], grecv_sem.at[c, row], r, col)
+        send(src, gath.at[c, row], zsend_sem.at[c, 0], grecv_sem.at[c, row], up, col, has_up)
+        send(src, gath.at[c, row], zsend_sem.at[c, 1], grecv_sem.at[c, row], down, col, has_down)
         x_send(c, row, 0, src)
+
+    for c in range(AHEAD):
+        own(c)
 
     wmine = pl.ds(pl.multiple_of(col * wr, wr), wr)
     for k, t in enumerate(q_to):
@@ -105,9 +116,16 @@
     lax.fori_loop(0, row_blk, make_dense, 0)
 
     def forward(c):
-        for n, r in enumerate(z_from):
-            arrived(gath.at[c, r], grecv_sem.at[c, r])
-            x_send(c, r, n + 1, gath.at[c, r])
+        for d in range(1, z_n):
+            for side in range(2):
+                r = row - d * x_n if side == 0 else row + d * x_n
+                here = z >= d if side == 0 else z + d < z_n
+                there = jnp.logical_and(here, has_up if side == 0 else has_down)
+                src = gath.at[c, r]
+                n = 2 * d + side - 1
+                pl.when(here)(functools.partial(arrived, src, grecv_sem.at[c, r]))
+                send(src, src, zsend_sem.at[c, n + 1], grecv_sem.at[c, r], up if side == 0 else down, col, there)
+                x_send(c, r, n, src, here)
 
     def w_forward():
         for k, t in enumerate(q_from):
@@ -174,22 +192,26 @@
         else:
             out_ref[...] = jnp.maximum(acc[...] + part, 0.0).astype(out_ref.dtype)
 
-    forward(0)
-    for step in range(1, CHUNKS + 4):
+    for step in range(CHUNKS + LATE + 2):
+        if step + AHEAD < CHUNKS:
+            own(step + AHEAD)
         if step < CHUNKS:
             forward(step)
-        if step == 2:
+        if step == 1:
             w_forward()
-        if 0 <= step - 1 < CHUNKS:
-            aggregate(step - 1)
-        if 0 <= step - 2 < CHUNKS:
-            pair_sum(step - 2)
-        if step == 3:
+        if 0 <= step - LATE < CHUNKS:
+            aggregate(step - LATE)
+        if 0 <= step - LATE - 1 < CHUNKS:
+            pair_sum(step - LATE - 1)
+        if step == LATE + 2:
             w_arrive()
-        if 0 <= step - 3 < CHUNKS:
-            finish(step - 3)
-    for copy in sends:
-        copy.wait_send()
+        if 0 <= step - LATE - 2 < CHUNKS:
+            finish(step - LATE - 2)
+    for copy, present in sends:
+        if present is None:
+            copy.wait_send()
+        else:
+            pl.when(present)(copy.wait_send)
 
 
 def solution(mesh):
@@ -223,8 +245,8 @@
                 pltpu.VMEM((CHUNKS, q_n, out_rows, fc), bf16),
                 pltpu.VMEM((out_rows, wide), f32),
                 dma((2 + CHUNKS,)),
-                dma((CHUNKS, max(1, z_n - 1))),
-                dma((CHUNKS, z_n, max(1, x_n - 1))),
+                dma((CHUNKS, 2 * z_n)),
+                dma((CHUNKS, 2 * z_n, max(1, x_n - 1))),
                 dma((CHUNKS, rows_n)),
                 dma((max(1, q_n - 1),)),
                 dma((q_n,)),
@@ -235,7 +257,7 @@
                 dma((CHUNKS, q_n)),
             ],
             compiler_params=pltpu.CompilerParams(
-                collective_id=0, has_side_effects=True, vmem_limit_bytes=48 * 1024 * 1024),
+                collective_id=0, has_side_effects=True, vmem_limit_bytes=63 * 1024 * 1024),
             cost_estimate=pl.CostEstimate(flops=flops, bytes_accessed=4 * 1024 * 1024, transcendentals=0),
         )(block_cols, tile_counts, features, weight, tile_values)
 

time: 47.8 us -> 42.5 us (0.89)
  local copies, waits for them, and re-layouts: 5.26 us -> 1.67 us
  Pallas kernels: 42.3 us -> 40.6 us
    unnamed x11 -> x1, local copies, waits for them, and re-layouts: 5.26 us -> 1.67 us
    pallas_call x1, Pallas kernels: 42.3 us -> 40.6 us  [body(): pl.pallas_call(functools.partial(kernel, rows_n, cols_n, x_n), out_shape=...]
where the time goes in v2:
time: 42.5 us; the launch traced here: 42.3 us
  Pallas kernels  40.6 us (96%)
  local copies, waits for them, and re-layouts  1.67 us (4%)
    pallas_call x1, Pallas kernels, body(): pl.pallas_call(functools.partial(kernel, rows_n, cols_n, x_n), out_shape=...  40.6 us
    unnamed x1, local copies, waits for them, and re-layouts  1.67 us

profile of v2, /device:TPU:0, one launch (start us, length us, event | category | flops | bytes accessed | tf_op | source)
XLA Modules:
  0.0 42.3 jit_solution(7524172751193605677)
XLA Ops:
  0.0 40.6 %shard_map.55 = bf16[128,1024]{1,0:T(8,128)(2,1)} custom-call(s32[1,1,4,8]{3,2,1,0:T(4,128)} %cols_ref.1, s32[1,1,4]{2,1,0:T(1,128)} %counts_ref.1, bf16[128,1024]{1,0:T(8,128)(2,1)} %feat_ref.1, bf16[256,1024]{1,0:T(8,128)(2,1)} %weight_ref.1, bf16[1,1,4,8,128,128]{5,4,3,2,1,0:T(8,128)(2,1)} %vals_ref.1), custom_call_target="tpu_custom_call" | custom-call | flops 1342177280 | bytes 4194304 | tf_op jit(solution)/shard_map/pallas_call | solution.py:231
  40.6 1.7 %copy.7 = bf16[128,1024]{1,0:T(8,128)(2,1)} copy(bf16[128,1024]{1,0:T(8,128)(2,1)} %shard_map.55) | data formatting | bytes 524288

commit v3 on v2

--- a/solution.py
+++ b/solution.py
@@ -9,8 +9,9 @@
 
 MESH = pl.DeviceIdType.MESH
 CHUNKS = 4
-AHEAD = 2
-LATE = 1
+AHEAD = 4
+LATE = 2
+WFWD = 4
 
 
 def kernel(rows_n, cols_n, x_n, cols_ref, counts_ref, feat_ref, weight_ref, vals_ref, out_ref,
@@ -31,6 +32,7 @@
     feat = feat_ref.shape[1]
     fc = feat // CHUNKS
     wr = weight_ref.shape[0]
+    wpart = weight_ref.shape[1] // CHUNKS
 
     has_up, has_down = z < z_n - 1, z > 0
     up, down = (z + 1) * x_n + x, (z - 1) * x_n + x
@@ -84,7 +86,8 @@
                  z * x_n + (x + d) % x_n, col, present)
 
     def own(c):
-        src = feat_ref.at[:, pl.ds(c * fc, fc)]
+        local[2 + c].wait()
+        src = gath.at[c, row]
         send(src, gath.at[c, row], zsend_sem.at[c, 0], grecv_sem.at[c, row], up, col, has_up)
         send(src, gath.at[c, row], zsend_sem.at[c, 1], grecv_sem.at[c, row], down, col, has_down)
         x_send(c, row, 0, src)
@@ -92,10 +95,14 @@
     for c in range(AHEAD):
         own(c)
 
-    wmine = pl.ds(pl.multiple_of(col * wr, wr), wr)
-    for k, t in enumerate(q_to):
-        send(weight_ref, wfull.at[wmine], wsend_sem.at[k], wrecv_sem.at[col], row, t * 2 + core)
-    send(weight_ref, wfull.at[wmine], wfwd_sem.at[0], wrecv_sem.at[col], row, sib)
+    def w_own(c):
+        lane = pl.ds(c * wpart, wpart)
+        mine = wfull.at[pl.ds(pl.multiple_of(col * wr, wr), wr), lane]
+        for k, t in enumerate(q_to):
+            send(weight_ref.at[:, lane], mine, wsend_sem.at[c, k], wrecv_sem.at[col], row, t * 2 + core)
+        if c == CHUNKS - 1:
+            mine = wfull.at[pl.ds(pl.multiple_of(col * wr, wr), wr)]
+            send(weight_ref, mine, wfwd_sem.at[0], wrecv_sem.at[col], row, sib)
 
     local[0].wait()
 
@@ -143,7 +150,6 @@
     per = max(1, min(q_n, 256 // out_rows))
 
     def aggregate(c):
-        local[2 + c].wait()
         for d in x_steps:
             for zz in range(z_n):
                 r = zz * x_n + (x + d) % x_n
@@ -196,14 +202,15 @@
         if step + AHEAD < CHUNKS:
             own(step + AHEAD)
         if step < CHUNKS:
+            w_own(step)
             forward(step)
-        if step == 1:
+        if step == WFWD:
             w_forward()
         if 0 <= step - LATE < CHUNKS:
             aggregate(step - LATE)
         if 0 <= step - LATE - 1 < CHUNKS:
             pair_sum(step - LATE - 1)
-        if step == LATE + 2:
+        if step == max(WFWD, LATE + 2):
             w_arrive()
         if 0 <= step - LATE - 2 < CHUNKS:
             finish(step - LATE - 2)
@@ -248,7 +255,7 @@
                 dma((CHUNKS, 2 * z_n)),
                 dma((CHUNKS, 2 * z_n, max(1, x_n - 1))),
                 dma((CHUNKS, rows_n)),
-                dma((max(1, q_n - 1),)),
+                dma((CHUNKS, max(1, q_n - 1))),
                 dma((q_n,)),
                 dma((cols_n,)),
                 dma((CHUNKS,)),

time: 42.5 us -> 42.1 us (level)
  no operation moved by 1% of the time
where the time goes in v3:
time: 42.1 us; the launch traced here: 41.9 us
  Pallas kernels  40.3 us (96%)
  local copies, waits for them, and re-layouts  1.67 us (4%)
    pallas_call x1, Pallas kernels, body(): pl.pallas_call(functools.partial(kernel, rows_n, cols_n, x_n), out_shape=...  40.3 us
    unnamed x1, local copies, waits for them, and re-layouts  1.67 us

profile of v3, /device:TPU:0, one launch (start us, length us, event | category | flops | bytes accessed | tf_op | source)
XLA Modules:
  0.0 41.9 jit_solution(1459998940685005771)
XLA Ops:
  0.0 40.3 %shard_map.55 = bf16[128,1024]{1,0:T(8,128)(2,1)} custom-call(s32[1,1,4,8]{3,2,1,0:T(4,128)} %cols_ref.1, s32[1,1,4]{2,1,0:T(1,128)} %counts_ref.1, bf16[128,1024]{1,0:T(8,128)(2,1)} %feat_ref.1, bf16[256,1024]{1,0:T(8,128)(2,1)} %weight_ref.1, bf16[1,1,4,8,128,128]{5,4,3,2,1,0:T(8,128)(2,1)} %vals_ref.1), custom_call_target="tpu_custom_call" | custom-call | flops 1342177280 | bytes 4194304 | tf_op jit(solution)/shard_map/pallas_call | solution.py:238
  40.3 1.7 %copy.7 = bf16[128,1024]{1,0:T(8,128)(2,1)} copy(bf16[128,1024]{1,0:T(8,128)(2,1)} %shard_map.55) | data formatting | bytes 524288
